TPU v7x, 512 devices: a whole 4x8x8 slice. The times are simulated.
512 devices in a mesh: wide: 32 (over x, y_lo, core), narrow: 16 (over z, y_hi).
Axes of the slice: x: 4, y: 8 (y_hi: 2, y_lo: 4; y = y_hi * 4 + y_lo), z: 8, core: 2. Of those that a mesh axis runs over, the one named last changes fastest.
Arguments:
- query_act: bfloat16 [64, 16384], P(None, 'wide'), may hold values from -6 to 6
- query_grad: bfloat16 [64, 16384], P(None, 'narrow'), may hold values from -6 to 6
- act_basis: bfloat16 [16384, 16384], P('wide', 'narrow'), may hold values from -0.046875 to 0.046875
- grad_basis: bfloat16 [16384, 16384], P('narrow', 'wide'), may hold values from -0.046875 to 0.046875
- eigenvalues: float32 [16384, 16384], P('wide', 'narrow'), may hold values from 0.1 to 10
- train_act: bfloat16 [64, 16384], P(None, 'narrow'), may hold values from -6 to 6
- train_grad: bfloat16 [64, 16384], P(None, 'wide'), may hold values from -6 to 6
Outputs:
- scores: float32 [64, 64], replicated
All inputs are finite; a program needn't handle non-finite values.
Results may differ from a plain program's by a relative error of at most 0.0057.
Values may be sent and summed in bfloat16 or wider, within the bound.
A program may use at most 64 MiB of HBM per device.

v0:
```python
import jax
import jax.numpy as jnp
from jax import lax
from jax.sharding import PartitionSpec as P

A = 16384
G = 16384


def split_up(array, dim, devices):
    dims = array.shape
    parts = array.reshape(*dims[:dim], devices, dims[dim] // devices, *dims[dim + 1 :])
    return jnp.moveaxis(parts, dim, 0)


def sum_at_owner(array, axis, dim):
    devices = lax.axis_size(axis)
    parts = lax.all_to_all(split_up(array, dim, devices), axis, 0, 0, tiled=True)
    return jnp.sum(parts, axis=0)


def sent_to_all(array, axis):
    copies = jnp.broadcast_to(array, (lax.axis_size(axis), *array.shape))
    return lax.all_to_all(copies, axis, split_axis=0, concat_axis=0, tiled=True)


def in_order(parts, dim):
    parts = jnp.moveaxis(parts, 0, dim)
    dims = parts.shape
    return parts.reshape(*dims[:dim], dims[dim] * dims[dim + 1], *dims[dim + 2 :])


def collect(array, axis, dim):
    parts = sent_to_all(array, axis)
    return in_order(parts, dim)


def over_copies(array, axis):
    return sent_to_all(array, axis).sum(axis=0)


def local_scores(rot_act, rot_grad, inverse, train_act, train_grad):
    count = rot_act.shape[0]
    blocks_act = rot_act.reshape(count // 8, 8, rot_act.shape[1])
    blocks_grad = rot_grad.reshape(count // 8, 8, rot_grad.shape[1])
    train_grad32 = train_grad.astype(jnp.float32)

    def one_block(items):
        block_act, block_grad = items
        pairs = (
            block_act.astype(jnp.float32)[:, None, :] * train_act.astype(jnp.float32)[None, :, :]
        ).astype(jnp.bfloat16)
        weighted = jnp.einsum("ij,btj->bti", inverse, pairs, preferred_element_type=jnp.float32)
        factor = block_grad.astype(jnp.float32)[:, None, :] * train_grad32[None, :, :]
        return jnp.sum(weighted * factor, axis=2)

    return lax.map(one_block, (blocks_act, blocks_grad)).reshape(count, train_act.shape[0])


def on_device(query_act, query_grad, act_basis, grad_basis, eigenvalues, train_act, train_grad):
    part_act = jnp.dot(query_act, act_basis, preferred_element_type=jnp.float32)
    part_grad = jnp.dot(query_grad, grad_basis, preferred_element_type=jnp.float32)
    share_act = sum_at_owner(part_act, "wide", 0).astype(jnp.bfloat16)
    share_grad = sum_at_owner(part_grad, "narrow", 0).astype(jnp.bfloat16)
    rot_act = collect(share_act, "wide", 0)
    rot_grad = collect(share_grad, "narrow", 0)
    inverse = (1.0 / eigenvalues).astype(jnp.bfloat16)
    partial_value = local_scores(rot_act, rot_grad, inverse, train_act, train_grad)
    column_piece = sum_at_owner(partial_value, "narrow", 1)
    column_piece = over_copies(column_piece, "wide")
    summed = collect(column_piece, "narrow", 1)
    return summed * float(A * G) ** (-0.5)


def solution(mesh):
    in_specs = (
        P(None, "wide"),
        P(None, "narrow"),
        P("wide", "narrow"),
        P("narrow", "wide"),
        P("wide", "narrow"),
        P(None, "narrow"),
        P(None, "wide"),
    )
    out_specs = P()
    return jax.shard_map(
        on_device, mesh=mesh, in_specs=in_specs, out_specs=out_specs, check_vma=False
    )
```

profile of v0, /device:TPU:1, one launch (start us, length us, event | category | flops | bytes accessed | tf_op | source)
XLA Modules:
  0.0 146.1 jit_solution(9887580874042606897)
XLA Ops:
  0.0 1.7 %fusion.5 = f32[64,512]{1,0:T(8,128)S(1)} fusion(bf16[64,1024]{1,0:T(8,128)(2,1)} %param.10, bf16[1024,512]{1,0:T(8,128)(2,1)} %param.12), kind=kOutput, calls=%fused_computation.17 | convolution fusion | flops 67108864 | bytes 1310720 | tf_op jit(solution)/shard_map/dot_general | solution.py:62
  1.7 0.7 reshape.28
  2.4 16.2 %all-to-all-start.2 = ((f32[16,4,512]{2,1,0:T(4,128)}), f32[16,4,512]{2,1,0:T(4,128)S(1)}, u32[]{:S(2)}, u32[]{:S(2)}) async-start(f32[16,4,512]{2,1,0:T(4,128)} %reshape.28), calls=%async_computation.2 | async-start | bytes 262144 | tf_op jit(solution)/shard_map/all_to_all | solution.py:18
  18.6 1.1 fusion.4
  19.8 0.8 reshape.27
  20.6 10.0 %all-to-all-done.2 = f32[16,4,512]{2,1,0:T(4,128)S(1)} async-done(((f32[16,4,512]{2,1,0:T(4,128)}), f32[16,4,512]{2,1,0:T(4,128)S(1)}, u32[]{:S(2)}, u32[]{:S(2)}) %all-to-all-start.2) | async-done | bytes 131104 | tf_op jit(solution)/shard_map/all_to_all | solution.py:18
  30.6 7.2 %all-to-all-start = ((f32[32,2,1024]{2,1,0:T(2,128)}), f32[32,2,1024]{2,1,0:T(2,128)S(1)}, u32[]{:S(2)}, u32[]{:S(2)}) async-start(f32[32,2,1024]{2,1,0:T(2,128)} %reshape.27), calls=%async_computation | async-start | bytes 524288 | tf_op jit(solution)/shard_map/all_to_all | solution.py:18
  37.8 11.2 %all-to-all-done = f32[32,2,1024]{2,1,0:T(2,128)S(1)} async-done(((f32[32,2,1024]{2,1,0:T(2,128)}), f32[32,2,1024]{2,1,0:T(2,128)S(1)}, u32[]{:S(2)}, u32[]{:S(2)}) %all-to-all-start) | async-done | bytes 262176 | tf_op jit(solution)/shard_map/all_to_all | solution.py:18
  49.1 0.6 broadcast_in_dim.25
  49.7 4.1 %all-to-all-start.3 = ((bf16[16,4,512]{2,1,0:T(4,128)(2,1)}), bf16[16,4,512]{2,1,0:T(4,128)(2,1)}, u32[]{:S(2)}, u32[]{:S(2)}) async-start(bf16[16,4,512]{2,1,0:T(4,128)(2,1)} %broadcast_in_dim.25), calls=%async_computation.3 | async-start | bytes 131072 | tf_op jit(solution)/shard_map/all_to_all | solution.py:24
  53.9 1.5 %convert_element_type.45 = f32[64,512]{1,0:T(8,128)} convert(bf16[64,512]{1,0:T(8,128)(2,1)} %param.15) | non-fusion elementwise | flops 32768 | bytes 196608 | tf_op jit(solution)/shard_map/convert_element_type | solution.py:46
  55.4 0.1 reduce_sum.45
  55.5 9.9 %all-to-all-done.3 = bf16[16,4,512]{2,1,0:T(4,128)(2,1)} async-done(((bf16[16,4,512]{2,1,0:T(4,128)(2,1)}), bf16[16,4,512]{2,1,0:T(4,128)(2,1)}, u32[]{:S(2)}, u32[]{:S(2)}) %all-to-all-start.3) | async-done | bytes 65568 | tf_op jit(solution)/shard_map/all_to_all | solution.py:24
  65.4 0.7 broadcast_in_dim.24
  66.1 4.7 %all-to-all-start.1 = ((bf16[32,2,1024]{2,1,0:T(2,128)(2,1)}), bf16[32,2,1024]{2,1,0:T(2,128)(2,1)S(1)}, u32[]{:S(2)}, u32[]{:S(2)}) async-start(bf16[32,2,1024]{2,1,0:T(2,128)(2,1)} %broadcast_in_dim.24), calls=%async_computation.1 | async-start | bytes 262144 | tf_op jit(solution)/shard_map/all_to_all | solution.py:24
  70.8 1.3 divide_convert_fusion
  72.1 0.9 reshape_reshape.10
  73.0 6.7 %all-to-all-done.1 = bf16[32,2,1024]{2,1,0:T(2,128)(2,1)S(1)} async-done(((bf16[32,2,1024]{2,1,0:T(2,128)(2,1)}), bf16[32,2,1024]{2,1,0:T(2,128)(2,1)S(1)}, u32[]{:S(2)}, u32[]{:S(2)}) %all-to-all-start.1) | async-done | bytes 131104 | tf_op jit(solution)/shard_map/all_to_all | solution.py:24
  79.7 21.5 %while.10 = (s32[]{:T(128)}, f32[8,8,64]{2,1,0:T(8,128)}, bf16[8,8,1024]{2,1,0:T(8,128)(2,1)S(1)}, bf16[64,1024]{1,0:T(8,128)(2,1)S(1)}, bf16[512,1024]{1,0:T(8,...) while((s32[]{:T(128)}, f32[8,8,64]{2,1,0:T(8,128)}, ...), condition=%wide.region_4.5_spmd, body=%wide.region_2.4_spmd.sunk | while | flops 538783232 | bytes 1966685 | solution.py:57
  79.8 2.0 %fusion.13 = f32[8,64]{1,0:T(8,128)S(1)} fusion(bf16[512,1024]{1,0:T(8,128)(2,1)} %get-tuple-element.120, f32[64,1024]{1,0:T(8,128)S(1)} %convert_element_type.54, f32[8,1024]{1,0:T(8,128)S(1)} %bitcast_convert_fusion.4, f32[64,512]{1,0:T(8,128)S(1)} %get-tuple-element.122, f32[8,512]{1,0:T(8,128)S(1)} %bitcast_convert_fusion.5), kind=kOutput, calls=%fused_computation.2.clone.1 | convolution fusion | flops 538705408 | bytes 1492992 | tf_op jit(solution)/shard_map/while/body/eval_jaxpr/ij,btj->bti/dot_general | solution.py:53
  81.8 0.6 bitcast_dynamic-update-slice_fusion.2
  82.5 2.1 %fusion.13 = f32[8,64]{1,0:T(8,128)S(1)} fusion(bf16[512,1024]{1,0:T(8,128)(2,1)} %get-tuple-element.120, f32[64,1024]{1,0:T(8,128)S(1)} %convert_element_type.54, f32[8,1024]{1,0:T(8,128)S(1)} %bitcast_convert_fusion.4, f32[64,512]{1,0:T(8,128)S(1)} %get-tuple-element.122, f32[8,512]{1,0:T(8,128)S(1)} %bitcast_convert_fusion.5), kind=kOutput, calls=%fused_computation.2.clone.1 | convolution fusion | flops 538705408 | bytes 1492992 | tf_op jit(solution)/shard_map/while/body/eval_jaxpr/ij,btj->bti/dot_general | solution.py:53
  84.5 0.6 bitcast_dynamic-update-slice_fusion.2
  85.2 2.1 %fusion.13 = f32[8,64]{1,0:T(8,128)S(1)} fusion(bf16[512,1024]{1,0:T(8,128)(2,1)} %get-tuple-element.120, f32[64,1024]{1,0:T(8,128)S(1)} %convert_element_type.54, f32[8,1024]{1,0:T(8,128)S(1)} %bitcast_convert_fusion.4, f32[64,512]{1,0:T(8,128)S(1)} %get-tuple-element.122, f32[8,512]{1,0:T(8,128)S(1)} %bitcast_convert_fusion.5), kind=kOutput, calls=%fused_computation.2.clone.1 | convolution fusion | flops 538705408 | bytes 1492992 | tf_op jit(solution)/shard_map/while/body/eval_jaxpr/ij,btj->bti/dot_general | solution.py:53
  87.2 0.6 bitcast_dynamic-update-slice_fusion.2
  87.8 2.0 %fusion.13 = f32[8,64]{1,0:T(8,128)S(1)} fusion(bf16[512,1024]{1,0:T(8,128)(2,1)} %get-tuple-element.120, f32[64,1024]{1,0:T(8,128)S(1)} %convert_element_type.54, f32[8,1024]{1,0:T(8,128)S(1)} %bitcast_convert_fusion.4, f32[64,512]{1,0:T(8,128)S(1)} %get-tuple-element.122, f32[8,512]{1,0:T(8,128)S(1)} %bitcast_convert_fusion.5), kind=kOutput, calls=%fused_computation.2.clone.1 | convolution fusion | flops 538705408 | bytes 1492992 | tf_op jit(solution)/shard_map/while/body/eval_jaxpr/ij,btj->bti/dot_general | solution.py:53
  89.9 0.6 bitcast_dynamic-update-slice_fusion.2
  90.5 2.1 %fusion.13 = f32[8,64]{1,0:T(8,128)S(1)} fusion(bf16[512,1024]{1,0:T(8,128)(2,1)} %get-tuple-element.120, f32[64,1024]{1,0:T(8,128)S(1)} %convert_element_type.54, f32[8,1024]{1,0:T(8,128)S(1)} %bitcast_convert_fusion.4, f32[64,512]{1,0:T(8,128)S(1)} %get-tuple-element.122, f32[8,512]{1,0:T(8,128)S(1)} %bitcast_convert_fusion.5), kind=kOutput, calls=%fused_computation.2.clone.1 | convolution fusion | flops 538705408 | bytes 1492992 | tf_op jit(solution)/shard_map/while/body/eval_jaxpr/ij,btj->bti/dot_general | solution.py:53
  92.6 0.6 bitcast_dynamic-update-slice_fusion.2
  93.2 2.0 %fusion.13 = f32[8,64]{1,0:T(8,128)S(1)} fusion(bf16[512,1024]{1,0:T(8,128)(2,1)} %get-tuple-element.120, f32[64,1024]{1,0:T(8,128)S(1)} %convert_element_type.54, f32[8,1024]{1,0:T(8,128)S(1)} %bitcast_convert_fusion.4, f32[64,512]{1,0:T(8,128)S(1)} %get-tuple-element.122, f32[8,512]{1,0:T(8,128)S(1)} %bitcast_convert_fusion.5), kind=kOutput, calls=%fused_computation.2.clone.1 | convolution fusion | flops 538705408 | bytes 1492992 | tf_op jit(solution)/shard_map/while/body/eval_jaxpr/ij,btj->bti/dot_general | solution.py:53
  95.3 0.6 bitcast_dynamic-update-slice_fusion.2
  95.9 2.1 %fusion.13 = f32[8,64]{1,0:T(8,128)S(1)} fusion(bf16[512,1024]{1,0:T(8,128)(2,1)} %get-tuple-element.120, f32[64,1024]{1,0:T(8,128)S(1)} %convert_element_type.54, f32[8,1024]{1,0:T(8,128)S(1)} %bitcast_convert_fusion.4, f32[64,512]{1,0:T(8,128)S(1)} %get-tuple-element.122, f32[8,512]{1,0:T(8,128)S(1)} %bitcast_convert_fusion.5), kind=kOutput, calls=%fused_computation.2.clone.1 | convolution fusion | flops 538705408 | bytes 1492992 | tf_op jit(solution)/shard_map/while/body/eval_jaxpr/ij,btj->bti/dot_general | solution.py:53
  98.0 0.6 bitcast_dynamic-update-slice_fusion.2
  98.6 2.1 %fusion.13 = f32[8,64]{1,0:T(8,128)S(1)} fusion(bf16[512,1024]{1,0:T(8,128)(2,1)} %get-tuple-element.120, f32[64,1024]{1,0:T(8,128)S(1)} %convert_element_type.54, f32[8,1024]{1,0:T(8,128)S(1)} %bitcast_convert_fusion.4, f32[64,512]{1,0:T(8,128)S(1)} %get-tuple-element.122, f32[8,512]{1,0:T(8,128)S(1)} %bitcast_convert_fusion.5), kind=kOutput, calls=%fused_computation.2.clone.1 | convolution fusion | flops 538705408 | bytes 1492992 | tf_op jit(solution)/shard_map/while/body/eval_jaxpr/ij,btj->bti/dot_general | solution.py:53
  100.6 0.6 bitcast_dynamic-update-slice_fusion.2
  101.2 0.9 copy.10
  102.2 0.1 reshape_reshape.11
  102.3 0.1 reshape.32
  102.4 13.9 %all_to_all.35 = f32[16,1,256]{2,1,0:T(1,128)S(1)} all-to-all(f32[16,1,256]{2,1,0:T(1,128)S(1)} %reshape.32), channel_id=1, replica_groups=mesh['wide'=32,'narrow'=16] {'narrow'}, dimensions={0} | all-to-all | bytes 32768 | tf_op jit(solution)/shard_map/all_to_all | solution.py:18
  116.3 0.5 broadcast.7
  116.8 0.7 reduce
  117.6 0.1 reshape.34
  117.7 12.0 %all_to_all.36 = f32[32,1,256]{2,1,0:T(1,128)S(1)} all-to-all(f32[32,1,256]{2,1,0:T(1,128)S(1)} %reshape.34), channel_id=1, replica_groups=mesh['wide'=32,'narrow'=16] {'wide'}, dimensions={0} | all-to-all | bytes 65536 | tf_op jit(solution)/shard_map/all_to_all | solution.py:24
  129.7 0.7 reduce.1
  130.6 0.1 reshape.36
  130.7 13.9 %all_to_all.37 = f32[16,1,256]{2,1,0:T(1,128)S(1)} all-to-all(f32[16,1,256]{2,1,0:T(1,128)S(1)} %reshape.36), channel_id=1, replica_groups=mesh['wide'=32,'narrow'=16] {'narrow'}, dimensions={0} | all-to-all | bytes 32768 | tf_op jit(solution)/shard_map/all_to_all | solution.py:24
  144.6 0.7 reduce.2
  145.4 0.7 copy.11
  (44 shorter events, 0.7 us)
Async XLA Ops:
  0.0 18.6 %copy-start = (bf16[512,1024]{1,0:T(8,128)(2,1)S(1)}, bf16[512,1024]{1,0:T(8,128)(2,1)}, u32[]{:S(2)}) copy-start(bf16[512,1024]{1,0:T(8,128)(2,1)} %param.11) | copy-start | bytes 3145732
  1.7 69.1 %copy-start.2 = (f32[512,1024]{1,0:T(8,128)S(1)}, f32[512,1024]{1,0:T(8,128)}, u32[]{:S(2)}) copy-start(f32[512,1024]{1,0:T(8,128)} %param.13) | copy-start | bytes 6291460
  2.4 28.2 %all-to-all-start.2 = ((f32[16,4,512]{2,1,0:T(4,128)}), f32[16,4,512]{2,1,0:T(4,128)S(1)}, u32[]{:S(2)}, u32[]{:S(2)}) async-start(f32[16,4,512]{2,1,0:T(4,128)} %reshape.28), calls=%async_computation.2 | async-start | bytes 262144 | tf_op jit(solution)/shard_map/all_to_all | solution.py:18
  30.6 18.5 %all-to-all-start = ((f32[32,2,1024]{2,1,0:T(2,128)}), f32[32,2,1024]{2,1,0:T(2,128)S(1)}, u32[]{:S(2)}, u32[]{:S(2)}) async-start(f32[32,2,1024]{2,1,0:T(2,128)} %reshape.27), calls=%async_computation | async-start | bytes 524288 | tf_op jit(solution)/shard_map/all_to_all | solution.py:18
  49.7 15.7 %all-to-all-start.3 = ((bf16[16,4,512]{2,1,0:T(4,128)(2,1)}), bf16[16,4,512]{2,1,0:T(4,128)(2,1)}, u32[]{:S(2)}, u32[]{:S(2)}) async-start(bf16[16,4,512]{2,1,0:T(4,128)(2,1)} %broadcast_in_dim.25), calls=%async_computation.3 | async-start | bytes 131072 | tf_op jit(solution)/shard_map/all_to_all | solution.py:24
  55.4 24.3 %copy-start.1 = (bf16[64,1024]{1,0:T(8,128)(2,1)S(1)}, bf16[64,1024]{1,0:T(8,128)(2,1)}, u32[]{:S(2)}) copy-start(bf16[64,1024]{1,0:T(8,128)(2,1)} %param.14) | copy-start | bytes 393220
  55.5 24.2 %copy-start.3 = (f32[64,512]{1,0:T(8,128)S(1)}, f32[64,512]{1,0:T(8,128)}, u32[]{:S(2)}) copy-start(f32[64,512]{1,0:T(8,128)} %convert_element_type.45) | copy-start | bytes 393220
  66.1 13.5 %all-to-all-start.1 = ((bf16[32,2,1024]{2,1,0:T(2,128)(2,1)}), bf16[32,2,1024]{2,1,0:T(2,128)(2,1)S(1)}, u32[]{:S(2)}, u32[]{:S(2)}) async-start(bf16[32,2,1024]{2,1,0:T(2,128)(2,1)} %broadcast_in_dim.24), calls=%async_computation.1 | async-start | bytes 262144 | tf_op jit(solution)/shard_map/all_to_all | solution.py:24
where the time goes:
time: 147 us; the launch traced here: 146 us
  blocking collectives  39.7 us (27%)
  waiting for transfers between devices  37.8 us (26%)
  starting transfers between devices  32.3 us (22%)
  matrix products  19.2 us (13%)
  local copies, waits for them, and re-layouts  11.5 us (8%)
  other arithmetic  5.31 us (4%)
    all_to_all x2, blocking collectives, sent_to_all(): return lax.all_to_all(copies, axis, split_axis=0, concat_axis=0, tiled=True)  25.9 us
    all_to_all x2, starting transfers between devices, sum_at_owner(): lax.all_to_all(split_up(array, dim, devices), axis, 0, 0, tiled=True)  23.4 us
    all_to_all x2, waiting for transfers between devices, sum_at_owner(): lax.all_to_all(split_up(array, dim, devices), axis, 0, 0, tiled=True)  21.2 us
    all_to_all x2, waiting for transfers between devices, sent_to_all(): return lax.all_to_all(copies, axis, split_axis=0, concat_axis=0, tiled=True)  16.6 us
    dot_general x8, matrix products, one_block(): jnp.einsum('ij,btj->bti', inverse, pairs, preferred_element_type=jnp.floa...  16.4 us
    all_to_all x1, blocking collectives, sum_at_owner(): lax.all_to_all(split_up(array, dim, devices), axis, 0, 0, tiled=True)  13.9 us
    all_to_all x2, starting transfers between devices, sent_to_all(): return lax.all_to_all(copies, axis, split_axis=0, concat_axis=0, tiled=True)  8.86 us
    dynamic_update_slice x8, local copies, waits for them, and re-layouts, local_scores(): lax.map(one_block, (blocks_act, blocks_grad))  4.8 us
  transfers between devices with their start and end apart: 4, of which 4 were waited for; matrix products, arithmetic and copies ran while one was open for 4% of the time, Pallas kernels for 0%

commit v1 on v0

v1 whole, which is shorter than its diff:
```python
import jax
import jax.numpy as jnp
from jax import lax
from jax.experimental import pallas as pl
from jax.experimental.pallas import tpu as pltpu
from jax.sharding import PartitionSpec as P

A = 16384
G = 16384
BF = jnp.bfloat16
F32 = jnp.float32
MESH = pl.DeviceIdType.MESH

CA, CG, CT, CI, HR, HG, ZR, VV, ZG, AX, AY, AZ, FC = range(13)
N_EXCHANGES = 13


def kernel(
    qa_h, qg_h, ab_h, gb_h, eig_h, ta_h, tg_h,
    out,
    qa, qg, ab, gb, eig, ta, tg,
    inv, keep, ca_s, ca_r, ha_s, ha_r, rot_a, cg_s, zg_s, zg_r, vg_s, vg_r, rot_g,
    raf, rgf, tgf, pairs, accs, s0, s1, s2, s3, xr, yr, zr, fr,
    load, send, recv,
):
    w, n = lax.axis_index("wide"), lax.axis_index("narrow")
    x, yl, c = w // 8, lax.rem(w // 2, 4), lax.rem(w, 2)
    z, yh = n // 2, lax.rem(n, 2)
    chip = w // 2
    partner = (w + 1 - 2 * c, n)
    across = (w, n + 1 - 2 * yh)

    def chip_peer(d):
        return (lax.rem(chip + d, 16) * 2 + c, n)

    def x_peer(d):
        return (lax.rem(w + 8 * d, 32), n)

    def y_peer(d):
        y = lax.rem(yh * 4 + yl + d, 8)
        return (x * 8 + lax.rem(y, 4) * 2 + c, z * 2 + y // 4)

    def z_peer(d):
        return (w, lax.rem(n + 2 * d, 16))

    mine, other = pl.ds(pl.multiple_of(c * 32, 32), 32), pl.ds(pl.multiple_of(32 - c * 32, 32), 32)
    loads = [
        (qa_h.at[mine], qa.at[pl.ds(0, 32)]),
        (qa_h.at[other], qa.at[pl.ds(32, 32)]),
        (ab_h, ab),
        (qg_h.at[mine], qg.at[pl.ds(0, 32)]),
        (qg_h.at[other], qg.at[pl.ds(32, 32)]),
        (gb_h, gb),
        (tg_h, tg.at[0]),
        (eig_h, eig),
        (ta_h, ta),
    ]
    loads = [pltpu.make_async_copy(s, d, load.at[i]) for i, (s, d) in enumerate(loads)]
    for one in loads:
        one.start()

    barrier = pltpu.get_barrier_semaphore()

    @pl.loop(1, 8)
    def _(d):
        pl.semaphore_signal(barrier, inc=1, device_id=z_peer(d), device_id_type=MESH)

    pl.semaphore_signal(barrier, inc=1, device_id=across, device_id_type=MESH)

    @pl.loop(1, 16)
    def _(d):
        pl.semaphore_signal(barrier, inc=1, device_id=chip_peer(d), device_id_type=MESH)

    pl.semaphore_signal(barrier, inc=1, device_id=partner, device_id_type=MESH)

    def remote(src, dst, i, peer):
        pltpu.make_async_remote_copy(
            src, dst, send.at[i], recv.at[i], device_id=peer, device_id_type=MESH
        ).start()

    def await_bytes(ref, sem):
        pltpu.make_async_copy(ref, ref, sem).wait()

    for i in range(3):
        loads[i].wait()
    part = jnp.dot(qa[...], ab[...], preferred_element_type=F32)
    for k in range(16):
        rows, cols = 16 * (k // 8), slice(128 * (k % 8), 128 * (k % 8) + 128)
        keep[k] = part[rows : rows + 16, cols]
        ca_s[k] = part[rows + 32 : rows + 48, cols].astype(BF)
    pl.semaphore_wait(barrier, 24)
    remote(ca_s, ca_r, CA, partner)
    for i in range(3, 6):
        loads[i].wait()
    part = jnp.dot(qg[...], gb[...], preferred_element_type=F32)
    for k in range(8):
        rows, cols = 16 * (k // 4), slice(128 * (k % 4), 128 * (k % 4) + 128)
        zg_s[k] = part[rows : rows + 16, cols].astype(BF)
        cg_s[k] = part[rows + 32 : rows + 48, cols].astype(BF)
    remote(cg_s, zg_s.at[pl.ds(8, 8)], CG, partner)

    await_bytes(ca_r, recv.at[CA])
    ha_s[...] = (keep[...] + ca_r[...].astype(F32)).astype(BF)

    @pl.loop(1, 16)
    def _(d):
        remote(ha_s.at[lax.rem(chip + d, 16)], ha_r.at[d - 1], HR, chip_peer(d))

    await_bytes(cg_s, recv.at[CG])

    @pl.loop(1, 8)
    def _(d):
        remote(zg_s.at[pl.ds(2 * lax.rem(z + d, 8), 2)], zg_r.at[d - 1], ZR, z_peer(d))

    loads[6].wait()
    remote(tg.at[0], tg.at[1], CT, partner)
    loads[7].wait()
    for k in range(2):
        inv[k] = (1.0 / eig[pl.ds(256 * k, 256), :]).astype(BF)
    remote(inv.at[pl.ds(0, 2)], inv.at[pl.ds(2, 2)], CI, partner)
    loads[8].wait()

    await_bytes(ha_r, recv.at[HR])
    rot_a[chip] = (ha_s[chip].astype(F32) + jnp.sum(ha_r[...].astype(F32), axis=0)).astype(BF)

    @pl.loop(1, 16)
    def _(d):
        remote(rot_a.at[chip], rot_a.at[chip], HG, chip_peer(d))

    await_bytes(zg_r, recv.at[ZR])
    own = pl.ds(2 * z, 2)
    total = zg_s[own].astype(F32) + jnp.sum(zg_r[...].astype(F32), axis=0)
    vg_s[...] = total.astype(BF)
    remote(vg_s, vg_r, VV, across)
    await_bytes(vg_r, recv.at[VV])
    rot_g[own] = (total + vg_r[...].astype(F32)).astype(BF)

    @pl.loop(1, 8)
    def _(d):
        remote(rot_g.at[own], rot_g.at[own], ZG, z_peer(d))

    await_bytes(tg.at[0], recv.at[CT])
    for k in range(2):
        tgf[:, 512 * k : 512 * k + 512] = tg[k].astype(F32)

    await_bytes(rot_a.at[pl.ds(0, 15)], recv.at[HG])
    for k in range(16):
        raf[16 * (k // 8) : 16 * (k // 8) + 16, 128 * (k % 8) : 128 * (k % 8) + 128] = rot_a[k].astype(F32)

    @pl.loop(0, 4)
    def _(b):
        for k in range(8):
            row = raf[pl.ds(b * 8 + k, 1), :]
            at = pl.multiple_of(b * 512 + k * 64, 64)
            for j in range(8):
                cols = slice(128 * j, 128 * j + 128)
                wide_row = jnp.broadcast_to(row[:, cols], (16, 128)).astype(BF)
                for t in range(4):
                    pairs[pl.ds(at + 16 * t, 16), cols] = wide_row * ta[16 * t : 16 * t + 16, cols]

    await_bytes(inv.at[pl.ds(0, 2)], recv.at[CI])
    await_bytes(rot_g.at[pl.ds(0, 14)], recv.at[ZG])
    for k in range(16):
        rows, cols = 16 * (k // 4 % 2), 512 * (k // 8) + 128 * (k % 4)
        rgf[rows : rows + 16, cols : cols + 128] = rot_g[k].astype(F32)

    accs[...] = jnp.zeros_like(accs)

    @pl.loop(0, 4)
    def _(b):
        weighted = lax.dot_general(
            pairs[...], inv[b], (((1,), (1,)), ((), ())), preferred_element_type=F32
        )
        cols = pl.ds(pl.multiple_of(b * 256, 256), 256)
        train = tgf[:, cols]
        for k in range(32):
            rows = slice(64 * k, 64 * k + 64)
            terms = weighted[rows] * train * rgf[pl.ds(k, 1), cols]
            accs[rows, :] += terms[:, :128] + terms[:, 128:]

    ones = jnp.ones((8, 128), BF)
    high = accs[...].astype(BF)
    low = (accs[...] - high.astype(F32)).astype(BF)
    last = (((1,), (1,)), ((), ()))
    sums = lax.dot_general(ones, high, last, preferred_element_type=F32) + lax.dot_general(
        ones, low, last, preferred_element_type=F32
    )
    for k in range(16):
        s0[k : k + 1, :] = sums[0:1, 128 * k : 128 * k + 128]

    for d in range(1, 4):
        remote(s0, xr.at[d - 1], AX, x_peer(d))
    await_bytes(xr, recv.at[AX])
    s1[...] = s0[...] + jnp.sum(xr[...], axis=0)

    @pl.loop(1, 8)
    def _(d):
        remote(s1, yr.at[d - 1], AY, y_peer(d))

    await_bytes(yr, recv.at[AY])
    s2[...] = s1[...] + jnp.sum(yr[...], axis=0)

    @pl.loop(1, 8)
    def _(d):
        remote(s2, zr.at[d - 1], AZ, z_peer(d))

    await_bytes(zr, recv.at[AZ])
    s3[...] = s2[...] + jnp.sum(zr[...], axis=0)
    remote(s3, fr, FC, partner)
    await_bytes(fr, recv.at[FC])
    out[c] = s3[...]
    out[1 - c] = fr[...]

    sent = {
        CA: ca_s, CG: cg_s, CT: tg.at[0], CI: inv.at[pl.ds(0, 2)], HR: ha_r, HG: ha_r, ZR: zg_r,
        VV: vg_s, ZG: rot_g.at[pl.ds(0, 14)], AX: xr, AY: yr, AZ: zr, FC: fr,
    }
    for i, ref in sent.items():
        await_bytes(ref, send.at[i])


def on_device(*operands):
    vm = pltpu.VMEM
    scratch = [
        vm((64, 512), BF), vm((64, 1024), BF), vm((512, 1024), BF), vm((1024, 512), BF),
        vm((512, 1024), F32), vm((64, 1024), BF), vm((2, 64, 512), BF),
        vm((4, 256, 1024), BF), vm((16, 16, 128), F32), vm((16, 16, 128), BF), vm((16, 16, 128), BF),
        vm((16, 16, 128), BF), vm((15, 16, 128), BF), vm((16, 16, 128), BF),
        vm((8, 16, 128), BF), vm((16, 16, 128), BF), vm((7, 2, 16, 128), BF),
        vm((2, 16, 128), BF), vm((2, 16, 128), BF), vm((16, 16, 128), BF),
        vm((32, 1024), F32), vm((32, 1024), F32), vm((64, 1024), F32),
        vm((2048, 1024), BF), vm((2048, 128), F32),
        vm((16, 128), F32), vm((16, 128), F32), vm((16, 128), F32), vm((16, 128), F32),
        vm((3, 16, 128), F32), vm((7, 16, 128), F32), vm((7, 16, 128), F32), vm((16, 128), F32),
        pltpu.SemaphoreType.DMA((9,)),
        pltpu.SemaphoreType.DMA((N_EXCHANGES,)),
        pltpu.SemaphoreType.DMA((N_EXCHANGES,)),
    ]
    scores = pl.pallas_call(
        kernel,
        out_shape=jax.ShapeDtypeStruct((2, 16, 128), F32),
        in_specs=[pl.BlockSpec(memory_space=pl.ANY)] * 7,
        out_specs=pl.BlockSpec(memory_space=pltpu.VMEM),
        scratch_shapes=scratch,
        compiler_params=pltpu.CompilerParams(
            collective_id=0, has_side_effects=True, vmem_limit_bytes=60 * 2**20
        ),
        name="influence",
    )(*operands)
    return scores.reshape(64, 64) * float(A * G) ** (-0.5)


def solution(mesh):
    in_specs = (
        P(None, "wide"),
        P(None, "narrow"),
        P("wide", "narrow"),
        P("narrow", "wide"),
        P("wide", "narrow"),
        P(None, "narrow"),
        P(None, "wide"),
    )
    return jax.shard_map(on_device, mesh=mesh, in_specs=in_specs, out_specs=P(), check_vma=False)
```

time: 147 us -> 53.3 us (0.36)
  Pallas kernels: 0 us -> 51.7 us
  blocking collectives: 39.7 us -> 0 us
  waiting for transfers between devices: 37.8 us -> 0 us
  starting transfers between devices: 32.3 us -> 0 us
  matrix products: 19.2 us -> 0 us
  local copies, waits for them, and re-layouts: 11.5 us -> 0.69 us
  other arithmetic: 5.31 us -> 0.72 us
    pallas_call x0 -> x1, Pallas kernels: none -> 51.7 us  [on_device(): pl.pallas_call(kernel, out_shape=jax.ShapeDtypeStruct((2, 16, 128), F32),...]
    all_to_all x3 -> x0, blocking collectives: 39.7 us -> none  [the longest x2 25.9 us: sent_to_all(): return lax.all_to_all(copies, axis, split_axis=0, concat_axis=0, tiled=True)]
    all_to_all x4 -> x0, waiting for transfers between devices: 37.8 us -> none  [the longest x2 21.2 us: sum_at_owner(): lax.all_to_all(split_up(array, dim, devices), axis, 0, 0, tiled=True)]
    all_to_all x4 -> x0, starting transfers between devices: 32.3 us -> none  [the longest x2 23.4 us: sum_at_owner(): lax.all_to_all(split_up(array, dim, devices), axis, 0, 0, tiled=True)]
    dot_general x10 -> x0, matrix products: 19.2 us -> none  [the longest x8 16.4 us: one_block(): jnp.einsum('ij,btj->bti', inverse, pairs, preferred_element_type=jnp.floa...]
    dynamic_update_slice x8 -> x0, local copies, waits for them, and re-layouts: 4.8 us -> none  [local_scores(): lax.map(one_block, (blocks_act, blocks_grad))]
    convert_element_type x26 -> x0, other arithmetic: 3.01 us -> none  [the longest x1 1.5 us: local_scores(): train_grad32 = train_grad.astype(jnp.float32)]
    all_to_all x3 -> x0, other arithmetic: 2.09 us -> none  [the longest x2 1.4 us: sent_to_all(): return lax.all_to_all(copies, axis, split_axis=0, concat_axis=0, tiled=True)]
  transfers between devices with their start and end apart: 4 -> 0, of which waited for: 4 -> 0; matrix products, arithmetic and copies ran while one was open for 4% -> 0% of each run, Pallas kernels for 0% -> 0%
where the time goes in v1:
time: 53.3 us; the launch traced here: 53.1 us
  Pallas kernels  51.7 us (97%)
  other arithmetic  0.72 us (1%)
  local copies, waits for them, and re-layouts  0.69 us (1%)
    pallas_call x1, Pallas kernels, on_device(): pl.pallas_call(kernel, out_shape=jax.ShapeDtypeStruct((2, 16, 128), F32),...  51.7 us

profile of v1, /device:TPU:1, one launch (start us, length us, event | category | flops | bytes accessed | tf_op | source)
XLA Modules:
  0.0 53.1 jit_solution(1615693902060293973)
XLA Ops:
  0.0 51.7 %influence.1 = f32[2,16,128]{2,1,0:T(8,128)} custom-call(bf16[64,512]{1,0:T(8,128)(2,1)} %qa_h.1, bf16[64,1024]{1,0:T(8,128)(2,1)} %qg_h.1, bf16[512,1024]{1,0:T(8,128)(2,1)} %ab_h.1, bf16[1024,512]{1,0:T(8,128)(2,1)} %gb_h.1, f32[512,1024]{1,0:T(8,128)} %eig_h.1, bf16[64,1024]{1,0:T(8,128)(2,1)} %ta_h.1, bf16[64,512]{1,0:T(8,128)(2,1)} %tg_h.1), custom_call_target="tpu_custom_call" | custom-call | tf_op jit(solution)/shard_map/influence/pallas_call | solution.py:239
  51.7 0.7 %broadcast_multiply_fusion = f32[2,16,128]{2,1,0:T(8,128)S(1)} fusion(f32[2,16,128]{2,1,0:T(8,128)} %influence.1), kind=kLoop, calls=%fused_computation | loop fusion | flops 4096 | bytes 32768 | tf_op jit(solution)/shard_map/mul | solution.py:250
  52.4 0.7 %mul.11 = f32[64,64]{1,0:T(8,128)} reshape(f32[2,16,128]{2,1,0:T(8,128)S(1)} %broadcast_multiply_fusion) | data formatting | bytes 32768 | tf_op jit(solution)/shard_map/mul | solution.py:250

commit v2 on v1

v2 whole, which is shorter than its diff:
```python
import jax
import jax.numpy as jnp
from jax import lax
from jax.experimental import pallas as pl
from jax.experimental.pallas import tpu as pltpu
from jax.sharding import PartitionSpec as P

A = 16384
G = 16384
BF = jnp.bfloat16
F32 = jnp.float32
MESH = pl.DeviceIdType.MESH

CA, CG, CT, CI, HR, HG, ZR, NG, AX, AY, AZ, FC = range(12)
N_EXCHANGES = 12
RING4 = (2, 1, 3)
RING8 = (4, 3, 5, 2, 6, 1, 7)


def kernel(
    qa_h, qg_h, ab_h, gb_h, eig_h, ta_h, tg_h,
    out,
    qa, qg, ab, gb, eig, ta, tg,
    inv, keep, ca_s, ca_r, ha_s, ha_r, rot_a, cg_s, zg_s, zg_r, rot_g,
    raf, rgf, tgf, pairs, first, accs, s0, s1, s2, s3, xr, yr, zr, fr,
    load, send, recv, ready,
):
    w, n = lax.axis_index("wide"), lax.axis_index("narrow")
    x, yl, c = w // 8, lax.rem(w // 2, 4), lax.rem(w, 2)
    z, yh = n // 2, lax.rem(n, 2)
    chip = w // 2
    partner = (w + 1 - 2 * c, n)
    across = (w, n + 1 - 2 * yh)

    owner = (yl == 1) | (yl == 2)

    def chip_at(dx, to_yl):
        return (lax.rem(x + dx, 4) * 8 + to_yl * 2 + c, n)

    def y_peer(d):
        y = lax.rem(yh * 4 + yl + d, 8)
        return (x * 8 + lax.rem(y, 4) * 2 + c, z * 2 + y // 4)

    def z_peer(d):
        return (w, lax.rem(n + 2 * d, 16))

    def narrow_peer(dz, dy):
        return (w, lax.rem(z + dz, 8) * 2 + lax.rem(yh + dy, 2))

    mine, other = pl.ds(pl.multiple_of(c * 32, 32), 32), pl.ds(pl.multiple_of(32 - c * 32, 32), 32)
    loads = [
        (qa_h.at[mine], qa.at[pl.ds(0, 32)]),
        (qa_h.at[other], qa.at[pl.ds(32, 32)]),
        (ab_h, ab),
        (qg_h.at[mine], qg.at[pl.ds(0, 32)]),
        (qg_h.at[other], qg.at[pl.ds(32, 32)]),
        (gb_h, gb),
        (tg_h, tg.at[0]),
        (eig_h, eig),
        (ta_h, ta),
    ]
    loads = [pltpu.make_async_copy(s, d, load.at[i]) for i, (s, d) in enumerate(loads)]
    for one in loads:
        one.start()

    barrier = pltpu.get_barrier_semaphore()

    def greet(peer):
        pl.semaphore_signal(barrier, inc=1, device_id=peer, device_id_type=MESH)

    for d in RING8:
        greet(z_peer(d))
    for d in RING4 + (0,):
        for e in (2, 1, 3, 0):
            if d or e:
                greet(chip_at(d, lax.rem(yl + e, 4)))
    greet(across)
    for e in (2, 1, 3):
        greet((w + 2 * (lax.rem(yl + e, 4) - yl), n + 1 - 2 * yh))
    greet(partner)

    def remote(src, dst, i, peer):
        pltpu.make_async_remote_copy(
            src, dst, send.at[i], recv.at[i], device_id=peer, device_id_type=MESH
        ).start()

    def await_bytes(ref, sem):
        pltpu.make_async_copy(ref, ref, sem).wait()

    for i in range(3):
        loads[i].wait()
    part = jnp.dot(qa[...], ab[...], preferred_element_type=F32)
    for k in range(16):
        rows, cols = 16 * (k // 8), slice(128 * (k % 8), 128 * (k % 8) + 128)
        keep[k] = part[rows : rows + 16, cols]
        ca_s[k] = part[rows + 32 : rows + 48, cols].astype(BF)
    pl.semaphore_wait(barrier, 27)
    pl.semaphore_signal(ready, inc=1, device_id=across, device_id_type=MESH)
    remote(ca_s, ca_r, CA, partner)
    for i in range(3, 6):
        loads[i].wait()
    part = jnp.dot(qg[...], gb[...], preferred_element_type=F32)
    for k in range(8):
        rows, cols = 16 * (k // 4), slice(128 * (k % 4), 128 * (k % 4) + 128)
        zg_s[k] = part[rows : rows + 16, cols].astype(BF)
        cg_s[k] = part[rows + 32 : rows + 48, cols].astype(BF)
    remote(cg_s, zg_s.at[pl.ds(8, 8)], CG, partner)

    await_bytes(ca_r, recv.at[CA])
    ha_s[...] = (keep[...] + ca_r[...].astype(F32)).astype(BF)
    for d in RING4 + (0,):
        for to in (1, 2):

            def to_owner(d=d, to=to):
                at = pl.ds(4 * lax.rem(x + d, 4) + 2 * to - 2, 2)
                slot = 4 * ((4 - d) % 4) + lax.rem(yl - to + 4, 4) - 1
                remote(ha_s.at[at], ha_r.at[slot], HR, chip_at(d, to))

            if d:
                to_owner()
            else:
                pl.when(yl != to)(to_owner)

    await_bytes(cg_s, recv.at[CG])
    for d in RING8:
        remote(zg_s.at[pl.ds(2 * lax.rem(z + d, 8), 2)], zg_r.at[d - 1], ZR, z_peer(d))

    loads[6].wait()
    remote(tg.at[0], tg.at[1], CT, partner)
    loads[7].wait()
    for k in range(2):
        inv[k] = (1.0 / eig[pl.ds(256 * k, 256), :]).astype(BF)
    remote(inv.at[pl.ds(0, 2)], inv.at[pl.ds(2, 2)], CI, partner)
    loads[8].wait()

    @pl.when(owner)
    def _():
        await_bytes(ha_r, recv.at[HR])
        at = pl.ds(4 * x + 2 * yl - 2, 2)
        rot_a[at] = (ha_s[at].astype(F32) + jnp.sum(ha_r[...].astype(F32), axis=0)).astype(BF)
        for d in RING4 + (0,):
            for e in (2, 1, 3, 0):
                if d or e:
                    remote(rot_a.at[at], rot_a.at[at], HG, chip_at(d, lax.rem(yl + e, 4)))

    await_bytes(zg_r, recv.at[ZR])
    own = pl.ds(2 * z, 2)
    held = pl.ds(16 * yh + 2 * z, 2)
    rot_g[held] = (zg_s[own].astype(F32) + jnp.sum(zg_r[...].astype(F32), axis=0)).astype(BF)
    pl.semaphore_wait(ready, 1)
    for e in (1, 0):
        for d in RING8 + (0,):
            if d or e:
                remote(rot_g.at[held], rot_g.at[held], NG, narrow_peer(d, e))

    await_bytes(tg.at[0], recv.at[CT])
    for k in range(2):
        tgf[:, 512 * k : 512 * k + 512] = tg[k].astype(F32)

    @pl.when(owner)
    def _():
        await_bytes(rot_a.at[pl.ds(0, 14)], recv.at[HG])

    @pl.when(jnp.logical_not(owner))
    def _():
        await_bytes(rot_a, recv.at[HG])

    for k in range(16):
        raf[16 * (k // 8) : 16 * (k // 8) + 16, 128 * (k % 8) : 128 * (k % 8) + 128] = rot_a[k].astype(F32)

    @pl.loop(0, 4)
    def _(b):
        for k in range(8):
            row = raf[pl.ds(b * 8 + k, 1), :]
            at = pl.multiple_of(b * 512 + k * 64, 64)
            for j in range(8):
                cols = slice(128 * j, 128 * j + 128)
                wide_row = jnp.broadcast_to(row[:, cols], (16, 128)).astype(BF)
                for t in range(4):
                    pairs[pl.ds(at + 16 * t, 16), cols] = wide_row * ta[16 * t : 16 * t + 16, cols]

    await_bytes(inv.at[pl.ds(0, 2)], recv.at[CI])

    def product(b):
        return lax.dot_general(
            pairs[...], inv[b], (((1,), (1,)), ((), ())), preferred_element_type=F32
        )

    def add_terms(b, weighted):
        cols = pl.ds(pl.multiple_of(b * 256, 256), 256)
        train = tgf[:, cols]
        for k in range(32):
            rows = slice(64 * k, 64 * k + 64)
            terms = weighted[rows] * train * rgf[pl.ds(k, 1), cols]
            accs[rows, :] += terms[:, :128] + terms[:, 128:]

    first[...] = product(0)
    await_bytes(rot_g.at[pl.ds(0, 30)], recv.at[NG])
    for k in range(16):
        rows, cols = 16 * (k // 4 % 2), 512 * (k // 8) + 128 * (k % 4)
        both = rot_g[k].astype(F32) + rot_g[16 + k].astype(F32)
        rgf[rows : rows + 16, cols : cols + 128] = both.astype(BF).astype(F32)

    accs[...] = jnp.zeros_like(accs)
    add_terms(0, first)

    @pl.loop(1, 4)
    def _(b):
        add_terms(b, product(b))

    ones = jnp.ones((8, 128), BF)
    high = accs[...].astype(BF)
    low = (accs[...] - high.astype(F32)).astype(BF)
    last = (((1,), (1,)), ((), ()))
    sums = lax.dot_general(ones, high, last, preferred_element_type=F32) + lax.dot_general(
        ones, low, last, preferred_element_type=F32
    )
    for k in range(16):
        s0[k : k + 1, :] = sums[0:1, 128 * k : 128 * k + 128]

    for d in RING4:
        remote(s0, xr.at[d - 1], AX, chip_at(d, yl))
    await_bytes(xr, recv.at[AX])
    s1[...] = s0[...] + jnp.sum(xr[...], axis=0)

    for d in RING8:
        remote(s1, yr.at[d - 1], AY, y_peer(d))

    await_bytes(yr, recv.at[AY])
    s2[...] = s1[...] + jnp.sum(yr[...], axis=0)

    for d in RING8:
        remote(s2, zr.at[d - 1], AZ, z_peer(d))

    await_bytes(zr, recv.at[AZ])
    s3[...] = (s2[...] + jnp.sum(zr[...], axis=0)) * float(A * G) ** (-0.5)
    remote(s3, fr, FC, partner)
    await_bytes(fr, recv.at[FC])
    for half, ref in ((c, s3), (1 - c, fr)):
        for k in range(32):
            out[pl.ds(32 * half + k, 1), :] = ref[k // 2 : k // 2 + 1, 64 * (k % 2) : 64 * (k % 2) + 64]

    sent = {
        CA: ca_s, CG: cg_s, CT: tg.at[0], CI: inv.at[pl.ds(0, 2)], ZR: zg_r,
        AX: xr, AY: yr, AZ: zr, FC: fr,
    }
    for i, ref in sent.items():
        await_bytes(ref, send.at[i])
    await_bytes(rot_g.at[pl.ds(0, 30)], send.at[NG])

    @pl.when(owner)
    def _():
        await_bytes(ha_s.at[pl.ds(0, 14)], send.at[HR])
        await_bytes(ha_r, send.at[HG])

    @pl.when(jnp.logical_not(owner))
    def _():
        await_bytes(ha_s, send.at[HR])


def on_device(*operands):
    vm = pltpu.VMEM
    scratch = [
        vm((64, 512), BF), vm((64, 1024), BF), vm((512, 1024), BF), vm((1024, 512), BF),
        vm((512, 1024), F32), vm((64, 1024), BF), vm((2, 64, 512), BF),
        vm((4, 256, 1024), BF), vm((16, 16, 128), F32), vm((16, 16, 128), BF), vm((16, 16, 128), BF),
        vm((16, 16, 128), BF), vm((15, 2, 16, 128), BF), vm((16, 16, 128), BF),
        vm((8, 16, 128), BF), vm((16, 16, 128), BF), vm((7, 2, 16, 128), BF),
        vm((32, 16, 128), BF),
        vm((32, 1024), F32), vm((32, 1024), F32), vm((64, 1024), F32),
        vm((2048, 1024), BF), vm((2048, 256), F32), vm((2048, 128), F32),
        vm((16, 128), F32), vm((16, 128), F32), vm((16, 128), F32), vm((16, 128), F32),
        vm((3, 16, 128), F32), vm((7, 16, 128), F32), vm((7, 16, 128), F32), vm((16, 128), F32),
        pltpu.SemaphoreType.DMA((9,)),
        pltpu.SemaphoreType.DMA((N_EXCHANGES,)),
        pltpu.SemaphoreType.DMA((N_EXCHANGES,)),
        pltpu.SemaphoreType.REGULAR,
    ]
    return pl.pallas_call(
        kernel,
        out_shape=jax.ShapeDtypeStruct((64, 64), F32),
        in_specs=[pl.BlockSpec(memory_space=pl.ANY)] * 7,
        out_specs=pl.BlockSpec(memory_space=pltpu.VMEM),
        scratch_shapes=scratch,
        compiler_params=pltpu.CompilerParams(
            collective_id=0, has_side_effects=True, vmem_limit_bytes=60 * 2**20
        ),
        name="influence",
    )(*operands)


def solution(mesh):
    in_specs = (
        P(None, "wide"),
        P(None, "narrow"),
        P("wide", "narrow"),
        P("narrow", "wide"),
        P("wide", "narrow"),
        P(None, "narrow"),
        P(None, "wide"),
    )
    return jax.shard_map(on_device, mesh=mesh, in_specs=in_specs, out_specs=P(), check_vma=False)
```

time: 53.3 us -> 50.3 us (0.944)
  Pallas kernels: 51.7 us -> 48.7 us
  other arithmetic: 0.72 us -> 0 us
  local copies, waits for them, and re-layouts: 0.69 us -> 1.38 us
    pallas_call x1, Pallas kernels: 51.7 us -> 48.7 us  [on_device(): pl.pallas_call(kernel, out_shape=jax.ShapeDtypeStruct((64, 64), F32), in_...]
    unnamed x0 -> x1, local copies, waits for them, and re-layouts: none -> 1.38 us
    mul x1 -> x0, other arithmetic: 0.72 us -> none  [on_device(): return scores.reshape(64, 64) * float(A * G) ** (-0.5)]
    mul x1 -> x0, local copies, waits for them, and re-layouts: 0.69 us -> none  [on_device(): return scores.reshape(64, 64) * float(A * G) ** (-0.5)]
where the time goes in v2:
time: 50.3 us; the launch traced here: 50.1 us
  Pallas kernels  48.7 us (97%)
  local copies, waits for them, and re-layouts  1.38 us (3%)
    pallas_call x1, Pallas kernels, on_device(): pl.pallas_call(kernel, out_shape=jax.ShapeDtypeStruct((64, 64), F32), in_...  48.7 us
    unnamed x1, local copies, waits for them, and re-layouts  1.38 us

profile of v2, /device:TPU:1, one launch (start us, length us, event | category | flops | bytes accessed | tf_op | source)
XLA Modules:
  0.0 50.1 jit_solution(10844830361091124532)
XLA Ops:
  0.0 48.7 %influence.1 = f32[64,64]{1,0:T(8,128)} custom-call(bf16[64,512]{1,0:T(8,128)(2,1)} %qa_h.1, bf16[64,1024]{1,0:T(8,128)(2,1)} %qg_h.1, bf16[512,1024]{1,0:T(8,128)(2,1)} %ab_h.1, bf16[1024,512]{1,0:T(8,128)(2,1)} %gb_h.1, f32[512,1024]{1,0:T(8,128)} %eig_h.1, bf16[64,1024]{1,0:T(8,128)(2,1)} %ta_h.1, bf16[64,512]{1,0:T(8,128)(2,1)} %tg_h.1), custom_call_target="tpu_custom_call" | custom-call | tf_op jit(solution)/shard_map/influence/pallas_call | solution.py:279
  48.7 1.4 %copy.9 = f32[64,64]{1,0:T(8,128)} copy(f32[64,64]{1,0:T(8,128)} %influence.1) | data formatting | bytes 32768

commit v3 on v2

--- a/solution.py
+++ b/solution.py
@@ -60,7 +60,7 @@
         (ta_h, ta),
     ]
     loads = [pltpu.make_async_copy(s, d, load.at[i]) for i, (s, d) in enumerate(loads)]
-    for one in loads:
+    for one in loads[:3]:
         one.start()
 
     barrier = pltpu.get_barrier_semaphore()
@@ -89,14 +89,16 @@
 
     for i in range(3):
         loads[i].wait()
+    for one in loads[3:]:
+        one.start()
     part = jnp.dot(qa[...], ab[...], preferred_element_type=F32)
     for k in range(16):
         rows, cols = 16 * (k // 8), slice(128 * (k % 8), 128 * (k % 8) + 128)
         keep[k] = part[rows : rows + 16, cols]
         ca_s[k] = part[rows + 32 : rows + 48, cols].astype(BF)
     pl.semaphore_wait(barrier, 27)
+    remote(ca_s, ca_r, CA, partner)
     pl.semaphore_signal(ready, inc=1, device_id=across, device_id_type=MESH)
-    remote(ca_s, ca_r, CA, partner)
     for i in range(3, 6):
         loads[i].wait()
     part = jnp.dot(qg[...], gb[...], preferred_element_type=F32)
@@ -105,7 +107,6 @@
         zg_s[k] = part[rows : rows + 16, cols].astype(BF)
         cg_s[k] = part[rows + 32 : rows + 48, cols].astype(BF)
     remote(cg_s, zg_s.at[pl.ds(8, 8)], CG, partner)
-
     await_bytes(ca_r, recv.at[CA])
     ha_s[...] = (keep[...] + ca_r[...].astype(F32)).astype(BF)
     for d in RING4 + (0,):
@@ -186,27 +187,26 @@
             pairs[...], inv[b], (((1,), (1,)), ((), ())), preferred_element_type=F32
         )
 
-    def add_terms(b, weighted):
-        cols = pl.ds(pl.multiple_of(b * 256, 256), 256)
-        train = tgf[:, cols]
-        for k in range(32):
-            rows = slice(64 * k, 64 * k + 64)
-            terms = weighted[rows] * train * rgf[pl.ds(k, 1), cols]
-            accs[rows, :] += terms[:, :128] + terms[:, 128:]
-
-    first[...] = product(0)
+    @pl.loop(0, 3)
+    def _(b):
+        first[b] = product(b)
+
     await_bytes(rot_g.at[pl.ds(0, 30)], recv.at[NG])
     for k in range(16):
         rows, cols = 16 * (k // 4 % 2), 512 * (k // 8) + 128 * (k % 4)
         both = rot_g[k].astype(F32) + rot_g[16 + k].astype(F32)
         rgf[rows : rows + 16, cols : cols + 128] = both.astype(BF).astype(F32)
 
-    accs[...] = jnp.zeros_like(accs)
-    add_terms(0, first)
-
-    @pl.loop(1, 4)
-    def _(b):
-        add_terms(b, product(b))
+    final = product(3)
+    for k in range(32):
+        rows = slice(64 * k, 64 * k + 64)
+        total = None
+        for b in range(4):
+            cols = slice(256 * b, 256 * b + 256)
+            terms = (first[b, rows] if b < 3 else final[rows]) * tgf[:, cols] * rgf[k : k + 1, cols]
+            terms = terms[:, :128] + terms[:, 128:]
+            total = terms if total is None else total + terms
+        accs[rows, :] = total
 
     ones = jnp.ones((8, 128), BF)
     high = accs[...].astype(BF)
@@ -236,9 +236,8 @@
     s3[...] = (s2[...] + jnp.sum(zr[...], axis=0)) * float(A * G) ** (-0.5)
     remote(s3, fr, FC, partner)
     await_bytes(fr, recv.at[FC])
-    for half, ref in ((c, s3), (1 - c, fr)):
-        for k in range(32):
-            out[pl.ds(32 * half + k, 1), :] = ref[k // 2 : k // 2 + 1, 64 * (k % 2) : 64 * (k % 2) + 64]
+    out[pl.ds(pl.multiple_of(16 * c, 16), 16), :] = s3[...]
+    out[pl.ds(pl.multiple_of(16 - 16 * c, 16), 16), :] = fr[...]
 
     sent = {
         CA: ca_s, CG: cg_s, CT: tg.at[0], CI: inv.at[pl.ds(0, 2)], ZR: zg_r,
@@ -268,7 +267,7 @@
         vm((8, 16, 128), BF), vm((16, 16, 128), BF), vm((7, 2, 16, 128), BF),
         vm((32, 16, 128), BF),
         vm((32, 1024), F32), vm((32, 1024), F32), vm((64, 1024), F32),
-        vm((2048, 1024), BF), vm((2048, 256), F32), vm((2048, 128), F32),
+        vm((2048, 1024), BF), vm((3, 2048, 256), F32), vm((2048, 128), F32),
         vm((16, 128), F32), vm((16, 128), F32), vm((16, 128), F32), vm((16, 128), F32),
         vm((3, 16, 128), F32), vm((7, 16, 128), F32), vm((7, 16, 128), F32), vm((16, 128), F32),
         pltpu.SemaphoreType.DMA((9,)),
@@ -276,9 +275,9 @@
         pltpu.SemaphoreType.DMA((N_EXCHANGES,)),
         pltpu.SemaphoreType.REGULAR,
     ]
-    return pl.pallas_call(
+    scores = pl.pallas_call(
         kernel,
-        out_shape=jax.ShapeDtypeStruct((64, 64), F32),
+        out_shape=jax.ShapeDtypeStruct((32, 128), F32),
         in_specs=[pl.BlockSpec(memory_space=pl.ANY)] * 7,
         out_specs=pl.BlockSpec(memory_space=pltpu.VMEM),
         scratch_shapes=scratch,
@@ -287,6 +286,7 @@
         ),
         name="influence",
     )(*operands)
+    return scores.reshape(64, 64)
 
 
 def solution(mesh):

time: 50.3 us -> 49.9 us (level)
    reshape x0 -> x1, local copies, waits for them, and re-layouts: none -> 1.4 us  [on_device(): return scores.reshape(64, 64)]
    unnamed x1 -> x0, local copies, waits for them, and re-layouts: 1.38 us -> none
where the time goes in v3:
time: 49.9 us; the launch traced here: 49.7 us
  Pallas kernels  48.3 us (97%)
  local copies, waits for them, and re-layouts  1.4 us (3%)
    pallas_call x1, Pallas kernels, on_device(): pl.pallas_call(kernel, out_shape=jax.ShapeDtypeStruct((32, 128), F32), in...  48.3 us
    reshape x1, local copies, waits for them, and re-layouts, on_device(): return scores.reshape(64, 64)  1.4 us

profile of v3, /device:TPU:1, one launch (start us, length us, event | category | flops | bytes accessed | tf_op | source)
XLA Modules:
  0.0 49.7 jit_solution(13284719410316553544)
XLA Ops:
  0.0 48.3 %influence.1 = f32[32,128]{1,0:T(8,128)} custom-call(bf16[64,512]{1,0:T(8,128)(2,1)} %qa_h.1, bf16[64,1024]{1,0:T(8,128)(2,1)} %qg_h.1, bf16[512,1024]{1,0:T(8,128)(2,1)} %ab_h.1, bf16[1024,512]{1,0:T(8,128)(2,1)} %gb_h.1, f32[512,1024]{1,0:T(8,128)} %eig_h.1, bf16[64,1024]{1,0:T(8,128)(2,1)} %ta_h.1, bf16[64,512]{1,0:T(8,128)(2,1)} %tg_h.1), custom_call_target="tpu_custom_call" | custom-call | tf_op jit(solution)/shard_map/influence/pallas_call | solution.py:278
  48.3 1.4 %reshape.3 = f32[64,64]{1,0:T(8,128)} reshape(f32[32,128]{1,0:T(8,128)} %influence.1) | data formatting | bytes 32768 | tf_op jit(solution)/shard_map/reshape | solution.py:289

commit v4 on v3

--- a/solution.py
+++ b/solution.py
@@ -277,7 +277,7 @@
     ]
     scores = pl.pallas_call(
         kernel,
-        out_shape=jax.ShapeDtypeStruct((32, 128), F32),
+        out_shape=pltpu.VMEM((32, 128), F32),
         in_specs=[pl.BlockSpec(memory_space=pl.ANY)] * 7,
         out_specs=pl.BlockSpec(memory_space=pltpu.VMEM),
         scratch_shapes=scratch,

time: 49.9 us -> 48.5 us (0.972)
  local copies, waits for them, and re-layouts: 1.4 us -> 0.69 us
  Pallas kernels: 48.3 us -> 47.7 us
    reshape x1, local copies, waits for them, and re-layouts: 1.4 us -> 0.69 us  [on_device(): return scores.reshape(64, 64)]
    pallas_call x1, Pallas kernels: 48.3 us -> 47.7 us  [on_device(): pl.pallas_call(kernel, out_shape=pltpu.VMEM((32, 128), F32), in_specs=[pl...]
where the time goes in v4:
time: 48.5 us; the launch traced here: 48.4 us
  Pallas kernels  47.7 us (98%)
  local copies, waits for them, and re-layouts  0.69 us (1%)
    pallas_call x1, Pallas kernels, on_device(): pl.pallas_call(kernel, out_shape=pltpu.VMEM((32, 128), F32), in_specs=[pl...  47.7 us

profile of v4, /device:TPU:1, one launch (start us, length us, event | category | flops | bytes accessed | tf_op | source)
XLA Modules:
  0.0 48.4 jit_solution(4497749210132326614)
XLA Ops:
  0.0 47.7 %influence.1 = f32[32,128]{1,0:T(8,128)S(1)} custom-call(bf16[64,512]{1,0:T(8,128)(2,1)} %qa_h.1, bf16[64,1024]{1,0:T(8,128)(2,1)} %qg_h.1, bf16[512,1024]{1,0:T(8,128)(2,1)} %ab_h.1, bf16[1024,512]{1,0:T(8,128)(2,1)} %gb_h.1, f32[512,1024]{1,0:T(8,128)} %eig_h.1, bf16[64,1024]{1,0:T(8,128)(2,1)} %ta_h.1, bf16[64,512]{1,0:T(8,128)(2,1)} %tg_h.1), custom_call_target="tpu_custom_call" | custom-call | tf_op jit(solution)/shard_map/influence/pallas_call | solution.py:278
  47.7 0.7 %reshape.3 = f32[64,64]{1,0:T(8,128)} reshape(f32[32,128]{1,0:T(8,128)S(1)} %influence.1) | data formatting | bytes 32768 | tf_op jit(solution)/shard_map/reshape | solution.py:289

commit v5 on v4

--- a/solution.py
+++ b/solution.py
@@ -134,6 +134,10 @@
     remote(inv.at[pl.ds(0, 2)], inv.at[pl.ds(2, 2)], CI, partner)
     loads[8].wait()
 
+    await_bytes(tg.at[0], recv.at[CT])
+    for k in range(2):
+        tgf[:, 512 * k : 512 * k + 512] = tg[k].astype(F32)
+
     @pl.when(owner)
     def _():
         await_bytes(ha_r, recv.at[HR])
@@ -154,10 +158,6 @@
             if d or e:
                 remote(rot_g.at[held], rot_g.at[held], NG, narrow_peer(d, e))
 
-    await_bytes(tg.at[0], recv.at[CT])
-    for k in range(2):
-        tgf[:, 512 * k : 512 * k + 512] = tg[k].astype(F32)
-
     @pl.when(owner)
     def _():
         await_bytes(rot_a.at[pl.ds(0, 14)], recv.at[HG])
@@ -169,25 +169,25 @@
     for k in range(16):
         raf[16 * (k // 8) : 16 * (k // 8) + 16, 128 * (k % 8) : 128 * (k % 8) + 128] = rot_a[k].astype(F32)
 
-    @pl.loop(0, 4)
-    def _(b):
-        for k in range(8):
-            row = raf[pl.ds(b * 8 + k, 1), :]
-            at = pl.multiple_of(b * 512 + k * 64, 64)
-            for j in range(8):
-                cols = slice(128 * j, 128 * j + 128)
-                wide_row = jnp.broadcast_to(row[:, cols], (16, 128)).astype(BF)
-                for t in range(4):
-                    pairs[pl.ds(at + 16 * t, 16), cols] = wide_row * ta[16 * t : 16 * t + 16, cols]
-
     await_bytes(inv.at[pl.ds(0, 2)], recv.at[CI])
+
+    for k in range(32):
+        row = raf[k : k + 1, :]
+        for j in range(8):
+            cols = slice(128 * j, 128 * j + 128)
+            wide_row = jnp.broadcast_to(row[:, cols], (16, 128)).astype(BF)
+            for t in range(4):
+                at = 64 * k + 16 * t
+                pairs[at : at + 16, cols] = wide_row * ta[16 * t : 16 * t + 16, cols]
 
     def product(b):
         return lax.dot_general(
             pairs[...], inv[b], (((1,), (1,)), ((), ())), preferred_element_type=F32
         )
 
-    @pl.loop(0, 3)
+    first[0] = product(0)
+
+    @pl.loop(1, 4)
     def _(b):
         first[b] = product(b)
 
@@ -197,16 +197,17 @@
         both = rot_g[k].astype(F32) + rot_g[16 + k].astype(F32)
         rgf[rows : rows + 16, cols : cols + 128] = both.astype(BF).astype(F32)
 
-    final = product(3)
-    for k in range(32):
-        rows = slice(64 * k, 64 * k + 64)
-        total = None
-        for b in range(4):
-            cols = slice(256 * b, 256 * b + 256)
-            terms = (first[b, rows] if b < 3 else final[rows]) * tgf[:, cols] * rgf[k : k + 1, cols]
-            terms = terms[:, :128] + terms[:, 128:]
-            total = terms if total is None else total + terms
-        accs[rows, :] = total
+    @pl.loop(0, 8)
+    def _(g):
+        for k in range(4):
+            rows = pl.ds(pl.multiple_of(256 * g + 64 * k, 64), 64)
+            total = None
+            for b in range(4):
+                cols = slice(256 * b, 256 * b + 256)
+                terms = first[b, rows] * tgf[:, cols] * rgf[pl.ds(4 * g + k, 1), cols]
+                terms = terms[:, :128] + terms[:, 128:]
+                total = terms if total is None else total + terms
+            accs[rows, :] = total
 
     ones = jnp.ones((8, 128), BF)
     high = accs[...].astype(BF)
@@ -267,7 +268,7 @@
         vm((8, 16, 128), BF), vm((16, 16, 128), BF), vm((7, 2, 16, 128), BF),
         vm((32, 16, 128), BF),
         vm((32, 1024), F32), vm((32, 1024), F32), vm((64, 1024), F32),
-        vm((2048, 1024), BF), vm((3, 2048, 256), F32), vm((2048, 128), F32),
+        vm((2048, 1024), BF), vm((4, 2048, 256), F32), vm((2048, 128), F32),
         vm((16, 128), F32), vm((16, 128), F32), vm((16, 128), F32), vm((16, 128), F32),
         vm((3, 16, 128), F32), vm((7, 16, 128), F32), vm((7, 16, 128), F32), vm((16, 128), F32),
         pltpu.SemaphoreType.DMA((9,)),

time: 48.5 us -> 48 us (0.990)
  Pallas kernels: 47.7 us -> 47.1 us
    pallas_call x1, Pallas kernels: 47.7 us -> 47.1 us  [on_device(): pl.pallas_call(kernel, out_shape=pltpu.VMEM((32, 128), F32), in_specs=[pl...]
where the time goes in v5:
time: 48 us; the launch traced here: 47.8 us
  Pallas kernels  47.1 us (98%)
  local copies, waits for them, and re-layouts  0.69 us (1%)
    pallas_call x1, Pallas kernels, on_device(): pl.pallas_call(kernel, out_shape=pltpu.VMEM((32, 128), F32), in_specs=[pl...  47.1 us

profile of v5, /device:TPU:1, one launch (start us, length us, event | category | flops | bytes accessed | tf_op | source)
XLA Modules:
  0.0 47.8 jit_solution(8138475634924806224)
XLA Ops:
  0.0 47.1 %influence.1 = f32[32,128]{1,0:T(8,128)S(1)} custom-call(bf16[64,512]{1,0:T(8,128)(2,1)} %qa_h.1, bf16[64,1024]{1,0:T(8,128)(2,1)} %qg_h.1, bf16[512,1024]{1,0:T(8,128)(2,1)} %ab_h.1, bf16[1024,512]{1,0:T(8,128)(2,1)} %gb_h.1, f32[512,1024]{1,0:T(8,128)} %eig_h.1, bf16[64,1024]{1,0:T(8,128)(2,1)} %ta_h.1, bf16[64,512]{1,0:T(8,128)(2,1)} %tg_h.1), custom_call_target="tpu_custom_call" | custom-call | tf_op jit(solution)/shard_map/influence/pallas_call | solution.py:279
  47.1 0.7 %reshape.3 = f32[64,64]{1,0:T(8,128)} reshape(f32[32,128]{1,0:T(8,128)S(1)} %influence.1) | data formatting | bytes 32768 | tf_op jit(solution)/shard_map/reshape | solution.py:290
